TPU v7x, 32 devices: a whole 2x2x4 slice. The times are simulated.
32 devices in a mesh: groups: 2 (over x), sector: 16 (over z, y, core).
Axes of the slice: x: 2, y: 2, z: 4, core: 2. Of those that a mesh axis runs over, the one named last changes fastest.
Arguments:
- psi_blocks: bfloat16 [1024, 64, 64], P(('groups', 'sector')), parts along dimension 0
- left_sector: int32 [1024], P(('groups', 'sector')), parts along dimension 0, may hold values from 0 to 127, as said below
- left_dims: int32 [256], P(('groups', 'sector')), parts along dimension 0, may hold values from 32 to 64
- right_sector: int32 [1024], P('groups'), parts along dimension 0, may hold values from 0 to 255, as said below
- right_dims: int32 [512], P('groups'), parts along dimension 0, may hold values from 32 to 64
- left_env: bfloat16 [256, 64, 2560], P(('groups', 'sector')), parts along dimension 0
- right_env: bfloat16 [512, 64, 2560], P(('groups', 'sector')), parts along dimension 0
Outputs:
- hpsi: float32 [1024, 64, 64], P(('groups', 'sector')), parts along dimension 0
- correction: float32 [1024, 64, 64], P(('groups', 'sector')), parts along dimension 0
- theta: float32 [2], P('groups'), parts along dimension 0
There are 2 independent parts, one for each index of `groups`. A program takes and returns all parts, laid end to end along the dimension named above; each array names one. Nothing has to cross between parts.
Inputs may be any that keep to these rules, and one draw needn't show every extreme that they name: Block g names a left sector of its own device: left_sector[g] // 8 == g // 32. `right_sector`: among the 32 blocks of one device at most 4 name right sectors of one owner (right sector s belongs to owner s // 16), and every device has an owner named by exactly 4 of its blocks. How many blocks an owner receives in all varies from owner to owner.
All inputs are finite; a program needn't handle non-finite values.
Results may differ from a plain program's by a relative error of at most 0.0047.
Values may be sent and summed in bfloat16 or wider, within the bound.
A program may use at most 192 MiB of HBM per device.

v0:
```python
import jax
import jax.numpy as jnp
from jax import lax
from jax.sharding import PartitionSpec as P


def body(psi_blocks, left_sector, left_dims, right_sector, right_dims, left_env, right_env):
    blocks = psi_blocks.shape[0]
    tile = psi_blocks.shape[1]
    bonds = left_env.shape[2] // tile
    left_count = left_env.shape[0]
    right_count = right_env.shape[0]
    owners = lax.axis_size("sector")
    device = lax.axis_index("sector")
    cap = (2 * blocks + owners - 1) // owners
    places = owners * cap
    table = right_sector.reshape(owners, blocks)
    owner_table = table // right_count
    order = jnp.arange(blocks, dtype=jnp.int32)
    before = order[None, :] < order[:, None]
    same = owner_table[:, :, None] == owner_table[:, None, :]
    rank_table = jnp.sum((same & before[None]).astype(jnp.int32), axis=2)
    own_sector = lax.dynamic_index_in_dim(table, device, 0, keepdims=False)
    own_owner = own_sector // right_count
    own_rank = lax.dynamic_index_in_dim(rank_table, device, 0, keepdims=False)
    target = own_owner * cap + own_rank
    slot_ids = jnp.arange(cap, dtype=jnp.int32)
    match = (owner_table[:, None, :] == device) & (
        rank_table[:, None, :] == slot_ids[None, :, None]
    )
    slot_sector = jnp.sum(jnp.where(match, table[:, None, :], 0), axis=2).reshape(places)
    slot_valid = jnp.any(match, axis=2).reshape(places)
    slot_local = jnp.where(slot_valid, slot_sector - device * right_count, 0)
    left_local = left_sector - device * left_count
    rows = jnp.sum(
        jnp.where(
            left_local[:, None] == jnp.arange(left_count, dtype=jnp.int32)[None, :],
            left_dims[None, :],
            0,
        ),
        axis=1,
    )
    cols = jnp.sum(
        jnp.where(
            own_sector[:, None] == jnp.arange(right_dims.shape[0], dtype=jnp.int32)[None, :],
            right_dims[None, :],
            0,
        ),
        axis=1,
    )
    place = jnp.arange(tile, dtype=jnp.int32)
    mask = (place[None, :, None] < rows[:, None, None]) & (
        place[None, None, :] < cols[:, None, None]
    )
    psi_used = jnp.where(mask, psi_blocks, jnp.zeros_like(psi_blocks))
    chosen_left = jnp.take(left_env, left_local, axis=0).reshape(blocks, tile, bonds, tile)
    partial_value = jnp.einsum(
        "bawc,bcd->bawd", chosen_left, psi_used, preferred_element_type=jnp.float32
    )
    partial_value = partial_value.astype(jnp.bfloat16).reshape(blocks, tile, bonds * tile)
    env_out = jnp.take(right_env, slot_local, axis=0)
    env_out = jnp.where(slot_valid[:, None, None], env_out, jnp.zeros((), jnp.bfloat16))
    env_in = lax.all_to_all(env_out, "sector", split_axis=0, concat_axis=0, tiled=True)
    chosen_right = jnp.take(env_in, target, axis=0)
    product_raw = jnp.einsum(
        "bax,bex->bae", partial_value, chosen_right, preferred_element_type=jnp.float32
    )
    hpsi = jnp.where(mask, product_raw, jnp.float32(0.0))
    psi_float = psi_used.astype(jnp.float32)
    inner = jnp.sum(psi_float * hpsi)
    weight = jnp.sum(psi_float * psi_float)
    total_cells = blocks * owners * tile * tile
    inner_all, weight_all = lax.psum((inner, weight), "sector")
    theta = inner_all / weight_all
    resid = hpsi - theta * psi_float
    spread = lax.psum(jnp.sum(resid * resid), "sector")
    scale = jnp.sqrt(spread / total_cells + 1e-06)
    return (hpsi, resid / scale, jnp.reshape(theta, (1,)))


def solution(mesh):
    placed = (
        P(("groups", "sector"), None, None),
        P(("groups", "sector")),
        P(("groups", "sector")),
        P("groups"),
        P("groups"),
        P(("groups", "sector"), None, None),
        P(("groups", "sector"), None, None),
    )
    return jax.shard_map(
        body,
        mesh=mesh,
        in_specs=placed,
        out_specs=(
            P(("groups", "sector"), None, None),
            P(("groups", "sector"), None, None),
            P("groups"),
        ),
        check_vma=False,
    )
```

profile of v0, /device:TPU:0, one launch (start us, length us, event | category | flops | bytes accessed | tf_op | source)
XLA Modules:
  0.0 588.0 jit_solution(16711824433111966843)
XLA Ops:
  0.7 0.9 reshape.300
  1.6 0.5 convert_reduce_fusion
  2.1 0.2 fusion.16
  2.2 0.2 select_reduce_fusion
  2.4 0.1 copy.15
  2.5 0.1 broadcast_in_dim.124
  2.7 0.1 select_n.140
  2.9 0.1 sub.48
  3.0 11.3 %gather_fusion.1 = bf16[64,64,2560]{2,1,0:T(8,128)(2,1)} fusion(bf16[16,64,2560]{2,1,0:T(8,128)(2,1)} %param.13, s32[1024]{0:T(1024)S(1)} %pad_clamp_fusion.1), kind=kCustom, calls=%fused_computation.1 | custom fusion | bytes 41943296 | tf_op jit(solution)/shard_map/jit(_take)/gather | solution.py:61
  14.2 18.4 %select_select_fusion = bf16[64,64,2560]{2,1,0:T(8,128)(2,1)} fusion(bf16[64,64,2560]{2,1,0:T(8,128)(2,1)} %gather_fusion.1, pred[64]{0:T(512)(128)(4,1)S(1)} %compare_and_fusion, pred[64]{0:T(512)(128)(4,1)S(1)} %broadcast_in_dim.124), kind=kLoop, calls=%fused_computation.5 | loop fusion | flops 20971520 | bytes 41943168 | tf_op jit(solution)/shard_map/jit(_where)/select_n | solution.py:62
  32.7 7.5 %all-to-all-start = ((bf16[64,64,2560]{2,1,0:T(8,128)(2,1)}), bf16[64,64,2560]{2,1,0:T(8,128)(2,1)}, u32[]{:S(2)}, u32[]{:S(2)}) async-start(bf16[64,64,2560]{2,1,0:T(8,128)(2,1)} %select_select_fusion), calls=%async_computation | async-start | bytes 41943040 | tf_op jit(solution)/shard_map/all_to_all | solution.py:63
  40.2 5.9 %gather_fusion = bf16[32,64,2560]{2,1,0:T(8,128)(2,1)} fusion(bf16[8,64,2560]{2,1,0:T(8,128)(2,1)S(1)} %copy-done, s32[1024]{0:T(1024)S(1)} %pad_clamp_fusion.2), kind=kCustom, calls=%fused_computation | custom fusion | bytes 20971648 | tf_op jit(solution)/shard_map/jit(_take)/gather | solution.py:56
  46.2 26.2 %gather.15 = bf16[32,64,40,64]{3,2,1,0:T(8,128)(2,1)} reshape(bf16[32,64,2560]{2,1,0:T(8,128)(2,1)} %gather_fusion) | data formatting | bytes 20971520 | tf_op jit(solution)/shard_map/jit(_take)/gather | solution.py:56
  72.5 0.2 select_reduce_fusion.1
  72.8 19.0 %fusion.2 = bf16[32,64,40,64]{3,1,2,0:T(8,128)(2,1)} fusion(bf16[32,64,40,64]{3,2,1,0:T(8,128)(2,1)} %gather.15, pred[32]{0:T(512)(128)(4,1)S(1)} %get-tuple-element.13, bf16[32,64,64]{2,1,0:T(8,128)(2,1)S(1)} %copy-done.2, pred[32,64]{1,0:T(8,128)(4,1)S(1)} %get-tuple-element.16, pred[32,64]{1,0:T(8,128)(4,1)S(1)} %get-tuple-element.17), kind=kOutput, calls=%fused_computation.7 | convolution fusion | flops 681836544 | bytes 21237792 | tf_op jit(solution)/shard_map/bawc,bcd->bawd/dot_general | solution.py:57
  91.8 24.9 %copy.14 = bf16[32,64,40,64]{3,2,1,0:T(8,128)(2,1)} copy(bf16[32,64,40,64]{3,1,2,0:T(8,128)(2,1)} %fusion.2) | data formatting | bytes 20971520 | tf_op jit(solution)/shard_map/convert_element_type | solution.py:60
  116.7 27.3 %reshape.301 = bf16[32,64,2560]{2,1,0:T(8,128)(2,1)} reshape(bf16[32,64,40,64]{3,2,1,0:T(8,128)(2,1)} %copy.14) | data formatting | bytes 20971520 | tf_op jit(solution)/shard_map/reshape | solution.py:60
  144.1 265.9 %all-to-all-done = bf16[64,64,2560]{2,1,0:T(8,128)(2,1)} async-done(((bf16[64,64,2560]{2,1,0:T(8,128)(2,1)}), bf16[64,64,2560]{2,1,0:T(8,128)(2,1)}, u32[]{:S(2)}, u32[]{:S(2)}) %all-to-all-start) | async-done | bytes 20971552 | tf_op jit(solution)/shard_map/all_to_all | solution.py:63
  409.9 12.9 %gather_fusion.2 = bf16[32,64,2560]{2,1,0:T(8,128)(2,1)} fusion(bf16[64,64,2560]{2,1,0:T(8,128)(2,1)} %all-to-all-done, s32[1024]{0:T(1024)S(1)} %pad_clamp_fusion), kind=kCustom, calls=%fused_computation.2 | custom fusion | bytes 20971648 | tf_op jit(solution)/shard_map/jit(_take)/gather | solution.py:64
  422.9 11.7 %fusion.11 = (f32[]{:T(128)}, f32[]{:T(128)}, f32[32,64,64]{2,1,0:T(8,128)}) fusion(bf16[32,64,64]{2,1,0:T(8,128)(2,1)S(1)} %copy-done.2, pred[32,64]{1,0:T(8,128)(4,1)S(1)} %get-tuple-element.16, pred[32,64]{1,0:T(8,128)(4,1)S(1)} %get-tuple-element.17, bf16[32,64,2560]{2,1,0:T(8,128)(2,1)} %reshape.301, bf16[32,64,2560]{2,1,0:T(8,128)(2,1)} %gather_fusion.2, ...), kind=kOutput, calls=%fused_computation.19 | convolution fusion | flops 677380096 | bytes 21762088 | tf_op jit(solution)/shard_map/bax,bex->bae/dot_general | solution.py:65
  434.6 115.7 %all-reduce = (f32[]{:T(128)}, f32[]{:T(128)}) all-reduce(f32[]{:T(128)} %get-tuple-element.4, f32[]{:T(128)} %get-tuple-element.3), channel_id=1, replica_groups=mesh['groups'=2,'sector'=16] {'sector'}, use_global_device_ids=true, to_apply=%region_6.7 | all-reduce | flops 2 | bytes 16 | tf_op jit(solution)/shard_map/psum | solution.py:73
  551.6 2.1 multiply_reduce_fusion
  553.7 30.1 %psum.23 = f32[]{:T(128)} all-reduce(f32[]{:T(128)} %multiply_reduce_fusion), channel_id=1, replica_groups=mesh['groups'=2,'sector'=16] {'sector'}, use_global_device_ids=true, to_apply=%region_10.11 | all-reduce | flops 1 | bytes 8 | tf_op jit(solution)/shard_map/psum | solution.py:76
  584.5 2.3 fusion.13
  (28 shorter events, 0.5 us)
Async XLA Ops:
  0.6 39.6 %copy-start = (bf16[8,64,2560]{2,1,0:T(8,128)(2,1)S(1)}, bf16[8,64,2560]{2,1,0:T(8,128)(2,1)}, u32[]{:S(2)}) copy-start(bf16[8,64,2560]{2,1,0:T(8,128)(2,1)} %param.12) | copy-start | bytes 7864324
  32.7 7.5 %copy-start.4 = (s32[32]{0:T(128)S(1)}, s32[32]{0:T(128)}, u32[]{:S(2)}) copy-start(s32[32]{0:T(128)} %param.8) | copy-start | bytes 388
  32.7 377.3 %all-to-all-start = ((bf16[64,64,2560]{2,1,0:T(8,128)(2,1)}), bf16[64,64,2560]{2,1,0:T(8,128)(2,1)}, u32[]{:S(2)}, u32[]{:S(2)}) async-start(bf16[64,64,2560]{2,1,0:T(8,128)(2,1)} %select_select_fusion), calls=%async_computation | async-start | bytes 41943040 | tf_op jit(solution)/shard_map/all_to_all | solution.py:63
  46.2 26.2 %copy-start.5 = (s32[8]{0:T(128)S(1)}, s32[8]{0:T(128)}, u32[]{:S(2)}) copy-start(s32[8]{0:T(128)} %param.9) | copy-start | bytes 100
  46.2 26.3 %copy-start.3 = (s32[256]{0:T(256)S(1)}, s32[256]{0:T(256)}, u32[]{:S(2)}) copy-start(s32[256]{0:T(256)} %param.11) | copy-start | bytes 3076
  46.2 26.6 %copy-start.2 = (bf16[32,64,64]{2,1,0:T(8,128)(2,1)S(1)}, bf16[32,64,64]{2,1,0:T(8,128)(2,1)}, u32[]{:S(2)}) copy-start(bf16[32,64,64]{2,1,0:T(8,128)(2,1)} %param.7) | copy-start | bytes 786436
  422.9 163.9 %copy-start.1 = (bf16[8,64,2560]{2,1,0:T(8,128)(2,1)S(1)}, bf16[8,64,2560]{2,1,0:T(8,128)(2,1)}, u32[]{:S(2)}) copy-start(bf16[8,64,2560]{2,1,0:T(8,128)(2,1)} %param.12) | copy-start | bytes 7864324
where the time goes:
time: 590 us; the launch traced here: 588 us
  waiting for transfers between devices  266 us (45%)
  blocking collectives  146 us (25%)
  local copies, waits for them, and re-layouts  110 us (19%)
  matrix products  30.8 us (5%)
  other arithmetic  24 us (4%)
  starting transfers between devices  7.48 us (1%)
    all_to_all x1, waiting for transfers between devices, body(): lax.all_to_all(env_out, 'sector', split_axis=0, concat_axis=0, tiled=True)  266 us
    psum x1, blocking collectives, body(): inner_all, weight_all = lax.psum((inner, weight), 'sector')  116 us
    gather x2, local copies, waits for them, and re-layouts, body(): jnp.take(left_env, left_local, axis=0).reshape(blocks, tile, bonds, tile)  32.2 us
    psum x1, blocking collectives, body(): spread = lax.psum(jnp.sum(resid * resid), 'sector')  30.1 us
    reshape x1, local copies, waits for them, and re-layouts, body(): partial_value.astype(jnp.bfloat16).reshape(blocks, tile, bonds * tile)  27.3 us
    convert_element_type x1, local copies, waits for them, and re-layouts, body(): partial_value.astype(jnp.bfloat16).reshape(blocks, tile, bonds * tile)  24.9 us
    dot_general x1, matrix products, body(): jnp.einsum('bawc,bcd->bawd', chosen_left, psi_used, preferred_element_typ...  19 us
    select_n x1, other arithmetic, body(): jnp.where(slot_valid[:, None, None], env_out, jnp.zeros((), jnp.bfloat16))  18.4 us
  transfers between devices with their start and end apart: 1, of which 1 were waited for; matrix products, arithmetic and copies ran while one was open for 18% of the time, Pallas kernels for 0%

commit v1 on v0

v1 whole, which is shorter than its diff:
```python
import functools

import jax
import jax.numpy as jnp
from jax import lax
from jax.experimental import pallas as pl
from jax.experimental.pallas import tpu as pltpu
from jax.sharding import PartitionSpec as P


def apply_kernel(li, ri, pi, ok, psi_ref, l_ref, r_ref, out_ref):
    s = pl.program_id(0)
    tile = psi_ref.shape[1]
    wide = 4 * tile
    chunks = l_ref.shape[2] // wide

    @pl.when(ok[s] > 0)
    def _():
        psi = psi_ref[0]
        row = jnp.concatenate([psi] * 4, axis=1)
        full = jnp.concatenate([row] * 4, axis=0)
        ia = lax.broadcasted_iota(jnp.int32, (wide, wide), 0) // tile
        ib = lax.broadcasted_iota(jnp.int32, (wide, wide), 1) // tile
        diag = jnp.where(ia == ib, full, jnp.zeros_like(full))
        acc = jnp.zeros((tile, tile), jnp.float32)
        for k in range(chunks):
            cut = slice(k * wide, (k + 1) * wide)
            t = jnp.dot(l_ref[0, :, cut], diag, preferred_element_type=jnp.float32)
            acc += lax.dot_general(
                t.astype(jnp.bfloat16), r_ref[0, :, cut], (((1,), (1,)), ((), ())),
                preferred_element_type=jnp.float32,
            )
        out_ref[0] = acc

    @pl.when(ok[s] == 0)
    def _():
        out_ref[0] = jnp.zeros_like(out_ref[0])


def apply_blocks(li, ri, pi, ok, psi, left, right):
    slots = li.shape[0]
    tile = psi.shape[1]
    width = left.shape[2]
    return pl.pallas_call(
        apply_kernel,
        grid_spec=pltpu.PrefetchScalarGridSpec(
            num_scalar_prefetch=4,
            grid=(slots,),
            in_specs=[
                pl.BlockSpec((1, tile, tile), lambda s, li, ri, pi, ok: (pi[s], 0, 0)),
                pl.BlockSpec((1, tile, width), lambda s, li, ri, pi, ok: (li[s], 0, 0)),
                pl.BlockSpec((1, tile, width), lambda s, li, ri, pi, ok: (ri[s], 0, 0)),
            ],
            out_specs=pl.BlockSpec((1, tile, tile), lambda s, li, ri, pi, ok: (s, 0, 0)),
        ),
        out_shape=jax.ShapeDtypeStruct((slots, tile, tile), jnp.float32),
        compiler_params=pltpu.CompilerParams(vmem_limit_bytes=32 * 1024 * 1024),
    )(li, ri, pi, ok, psi, left, right)


def body(psi_blocks, left_sector, left_dims, right_sector, right_dims, left_env, right_env):
    blocks, tile = psi_blocks.shape[:2]
    left_count = left_env.shape[0]
    right_count = right_env.shape[0]
    owners = lax.axis_size("sector")
    device = lax.axis_index("sector")
    cap = (2 * blocks + owners - 1) // owners
    q = 4
    p = owners // q
    slots = min(q * cap, blocks)
    along_z = [[z * q + y for z in range(p)] for y in range(q)]
    along_y = [[z * q + y for y in range(q)] for z in range(p)]
    my_z, my_y = device // q, device % q

    left_local = left_sector - device * left_count
    table = right_sector.reshape(owners, blocks)
    own_sector = lax.dynamic_index_in_dim(table, device, 0, keepdims=False)
    rows = jnp.sum(
        jnp.where(left_local[:, None] == jnp.arange(left_count, dtype=jnp.int32)[None, :],
                  left_dims[None, :], 0), axis=1)
    cols = jnp.sum(
        jnp.where(own_sector[:, None] == jnp.arange(right_dims.shape[0], dtype=jnp.int32)[None, :],
                  right_dims[None, :], 0), axis=1)
    place = jnp.arange(tile, dtype=jnp.int32)
    mask = (place[None, :, None] < rows[:, None, None]) & (
        place[None, None, :] < cols[:, None, None])
    psi_used = jnp.where(mask, psi_blocks, jnp.zeros_like(psi_blocks))

    left_all = lax.all_gather(left_env, "sector", axis_index_groups=along_z, tiled=True)
    right_all = lax.all_gather(right_env, "sector", axis_index_groups=along_y, tiled=True)
    psi_all = lax.all_gather(psi_used, "sector", axis_index_groups=along_z, tiled=True)
    ids_all = lax.all_gather(left_local, "sector", axis_index_groups=along_z, tiled=True)

    line = lax.dynamic_index_in_dim(table.reshape(p, q, blocks), my_y, 1, keepdims=False)
    goal = line // (right_count * q)
    order = jnp.arange(blocks, dtype=jnp.int32)
    same = (goal[:, :, None] == goal[:, None, :]) & (order[None, None, :] < order[None, :, None])
    rank = jnp.sum(same.astype(jnp.int32), axis=2)
    match = (goal[:, None, :] == my_z) & (
        rank[:, None, :] == jnp.arange(slots, dtype=jnp.int32)[None, :, None])

    def pick(values):
        return jnp.sum(jnp.where(match, values, 0), axis=2).reshape(p * slots)

    ok = pick(jnp.ones((p, 1, blocks), jnp.int32))
    base = jnp.arange(p, dtype=jnp.int32)[:, None, None]
    pi = pick(base * blocks + order[None, None, :])
    li = pick(base * left_count + ids_all.reshape(p, 1, blocks))
    ri = pick(line[:, None, :] - my_z * (q * right_count))
    out = apply_blocks(li, ri, pi, ok, psi_all, left_all, right_all)
    back = lax.all_to_all(out, "sector", split_axis=0, concat_axis=0, tiled=True,
                          axis_index_groups=along_z)
    own_rank = lax.dynamic_index_in_dim(rank, my_z, 0, keepdims=False)
    target = (own_sector // (right_count * q)) * slots + own_rank
    hpsi = jnp.where(mask, jnp.take(back, target, axis=0), jnp.float32(0.0))

    psi_float = psi_used.astype(jnp.float32)
    ph = jnp.sum(psi_float * hpsi)
    pp = jnp.sum(psi_float * psi_float)
    local = jnp.where(pp > 0, ph / jnp.where(pp > 0, pp, 1.0), 0.0)
    rest = hpsi - local * psi_float
    ss = jnp.sum(rest * rest)
    sums = lax.all_gather(jnp.stack([ph, pp, ss, local]), "sector")
    theta = jnp.sum(sums[:, 0]) / jnp.sum(sums[:, 1])
    gap = sums[:, 3] - theta
    spread = jnp.sum(sums[:, 2] + gap * gap * sums[:, 1])
    resid = hpsi - theta * psi_float
    scale = jnp.sqrt(spread / (blocks * owners * tile * tile) + 1e-06)
    return (hpsi, resid / scale, jnp.reshape(theta, (1,)))


def solution(mesh):
    placed = (
        P(("groups", "sector"), None, None),
        P(("groups", "sector")),
        P(("groups", "sector")),
        P("groups"),
        P("groups"),
        P(("groups", "sector"), None, None),
        P(("groups", "sector"), None, None),
    )
    return jax.shard_map(
        body,
        mesh=mesh,
        in_specs=placed,
        out_specs=(
            P(("groups", "sector"), None, None),
            P(("groups", "sector"), None, None),
            P("groups"),
        ),
        check_vma=False,
    )
```

time: 590 us -> 526 us (0.89)
  waiting for transfers between devices: 266 us -> 379 us
  blocking collectives: 146 us -> 39.5 us
  local copies, waits for them, and re-layouts: 110 us -> 16.2 us
  matrix products: 30.8 us -> 0 us
  Pallas kernels: 0 us -> 25.9 us
  starting transfers between devices: 7.48 us -> 26 us
  between operations: 3.94 us -> 20.4 us
    all_gather x0 -> x3, waiting for transfers between devices: none -> 352 us  [the longest x1 184 us: body(): lax.all_gather(left_env, 'sector', axis_index_groups=along_z, tiled=True)]
    all_to_all x1, waiting for transfers between devices: 266 us -> 25.8 us  [body(): lax.all_to_all(out, 'sector', split_axis=0, concat_axis=0, tiled=True, ax...]
    psum x2 -> x0, blocking collectives: 146 us -> none  [the longest x1 116 us: body(): inner_all, weight_all = lax.psum((inner, weight), 'sector')]
    gather x4 -> x1, local copies, waits for them, and re-layouts: 56.4 us -> 1.59 us  [body(): hpsi = jnp.where(mask, jnp.take(back, target, axis=0), jnp.float32(0.0))]
    unnamed x0 -> x2, blocking collectives: none -> 39.5 us
    dot_general x2 -> x0, matrix products: 30.8 us -> none  [the longest x1 19 us: body(): jnp.einsum('bawc,bcd->bawd', chosen_left, psi_used, preferred_element_typ...]
    reshape x1 -> x5, local copies, waits for them, and re-layouts: 27.3 us -> 0.41 us  [the longest x4 0.33 us: pick(): return jnp.sum(jnp.where(match, values, 0), axis=2).reshape(p * slots)]
    pallas_call x0 -> x1, Pallas kernels: none -> 25.9 us  [apply_blocks(): pl.pallas_call(apply_kernel, grid_spec=pltpu.PrefetchScalarGridSpec(num_s...]
  transfers between devices with their start and end apart: 1 -> 4, of which waited for: 1 -> 4; matrix products, arithmetic and copies ran while one was open for 18% -> 0% of each run, Pallas kernels for 0% -> 0%
where the time goes in v1:
time: 526 us; the launch traced here: 525 us
  waiting for transfers between devices  379 us (72%)
  blocking collectives  39.5 us (8%)
  starting transfers between devices  26 us (5%)
  Pallas kernels  25.9 us (5%)
  between operations  20.4 us (4%)
  other arithmetic  18.3 us (3%)
  local copies, waits for them, and re-layouts  16.2 us (3%)
    all_gather x1, waiting for transfers between devices, body(): lax.all_gather(left_env, 'sector', axis_index_groups=along_z, tiled=True)  184 us
    all_gather x1, waiting for transfers between devices, body(): lax.all_gather(right_env, 'sector', axis_index_groups=along_y, tiled=True)  131 us
    unnamed x2, blocking collectives  39.5 us
    all_gather x1, waiting for transfers between devices, body(): lax.all_gather(psi_used, 'sector', axis_index_groups=along_z, tiled=True)  36.4 us
    pallas_call x1, Pallas kernels, apply_blocks(): pl.pallas_call(apply_kernel, grid_spec=pltpu.PrefetchScalarGridSpec(num_s...  25.9 us
    all_to_all x1, starting transfers between devices, body(): lax.all_to_all(out, 'sector', split_axis=0, concat_axis=0, tiled=True, ax...  25.9 us
    all_to_all x1, waiting for transfers between devices, body(): lax.all_to_all(out, 'sector', split_axis=0, concat_axis=0, tiled=True, ax...  25.8 us
    unnamed x17, local copies, waits for them, and re-layouts  12.1 us
  transfers between devices with their start and end apart: 4, of which 4 were waited for; matrix products, arithmetic and copies ran while one was open for 0% of the time, Pallas kernels for 0%

profile of v1, /device:TPU:0, one launch (start us, length us, event | category | flops | bytes accessed | tf_op | source)
XLA Modules:
  0.0 525.5 jit_solution(3714375645444638668)
XLA Ops:
  7.3 0.8 reshape.281
  8.0 0.8 reshape_reshape.3
  8.8 1.2 dynamic-slice
  10.7 0.8 fusion.17
  12.5 0.9 select_reduce_fusion.4
  13.4 2.2 and_select_fusion.1
  17.1 9.9 %all-reduce = s32[128]{0:T(128)S(1)} all-reduce(s32[128]{0:T(128)S(1)} %get-tuple-element.14), channel_id=1, replica_groups={{0,4,8,12},{1,5,9,13},{2,6,10,14},{3,7,11,15},{16,20,24,28},{17,21,25,2..., use_global_device_ids=true, to_apply=%add | all-reduce | flops 128 | bytes 1024
  28.0 36.4 %all-gather.5.cloned.1.call-done.psi_ref = bf16[128,64,64]{2,1,0:T(8,128)(2,1)} async-done(((bf16[32,64,64]{2,1,0:T(8,128)(2,1)}), bf16[128,64,64]{2,1,0:T(8,128)(2,1)}) %all-gather.5.cloned.1.call-update) | async-done | bytes 1048592 | tf_op jit(solution)/shard_map/all_gather | solution.py:91
  64.4 184.2 %all-gather.7.cloned.1.call-done.l_ref = bf16[32,64,2560]{2,1,0:T(8,128)(2,1)} async-done(((bf16[8,64,2560]{2,1,0:T(8,128)(2,1)}), bf16[32,64,2560]{2,1,0:T(8,128)(2,1)}) %all-gather.7.cloned.1.call-update) | async-done | bytes 10485776 | tf_op jit(solution)/shard_map/all_gather | solution.py:89
  248.7 131.4 %all-gather.9.cloned.1.call-done.r_ref = bf16[64,64,2560]{2,1,0:T(8,128)(2,1)} async-done(((bf16[16,64,2560]{2,1,0:T(8,128)(2,1)}), bf16[64,64,2560]{2,1,0:T(8,128)(2,1)}) %all-gather.9.cloned.1.call-update) | async-done | bytes 20971536 | tf_op jit(solution)/shard_map/all_gather | solution.py:90
  380.1 4.0 copy-done
  384.1 1.6 copy-done.1
  385.6 25.9 %shard_map.94 = f32[64,64,64]{2,1,0:T(8,128)S(1)} custom-call(s32[64]{0:T(128)S(1)} %reshape.283.li, s32[64]{0:T(128)S(1)} %reshape.284.ri, s32[64]{0:T(128)S(1)} %reshape.285.pi, s32[64]{0:T(128)S(1)} %reshape.286.ok, bf16[128,64,64]{2,1,0:T(8,128)(2,1)S(1)} %copy-done.1, bf16[32,64,2560]{2,1,0:T(8,128)(2,1)S(1)} %copy-done, ...), custom_call_target="tpu_custom_call" | custom-call | tf_op jit(solution)/shard_map/pallas_call | solution.py:44
  411.5 2.4 reshape.307
  414.0 25.9 %all-to-all-start = ((f32[4,1,65536]{2,1,0:T(1,128)}), f32[4,1,65536]{2,1,0:T(1,128)S(1)}, u32[]{:S(2)}, u32[]{:S(2)}) async-start(f32[4,1,65536]{2,1,0:T(1,128)} %reshape.307), calls=%async_computation | async-start | bytes 2097152 | tf_op jit(solution)/shard_map/all_to_all | solution.py:111
  441.1 25.8 %all-to-all-done = f32[4,1,65536]{2,1,0:T(1,128)S(1)} async-done(((f32[4,1,65536]{2,1,0:T(1,128)}), f32[4,1,65536]{2,1,0:T(1,128)S(1)}, u32[]{:S(2)}, u32[]{:S(2)}) %all-to-all-start) | async-done | bytes 1048608 | tf_op jit(solution)/shard_map/all_to_all | solution.py:111
  467.4 4.7 reduce.3
  472.1 2.3 reshape.308
  474.3 1.6 gather_fusion
  475.9 2.3 fusion
  480.3 1.1 fusion.4
  481.4 2.1 maximum_dynamic-update-slice_fusion
  483.6 29.5 %all-reduce.1 = f32[64]{0:T(128)S(1)} all-reduce(f32[64]{0:T(128)S(1)} %maximum_dynamic-update-slice_fusion), channel_id=2, replica_groups=mesh['groups'=2,'sector'=16] {'sector'}, use_global_device_ids=true, to_apply=%add.1 | all-reduce | flops 64 | bytes 512
  516.6 1.2 fusion.6
  (42 shorter events, 6.1 us)
Async XLA Ops:
  7.2 57.3 %all-gather.5.cloned.1.call-start = ((), (), s32[]{:S(2)}) async-start(), calls=%async_computation.1 | async-start | bytes 2621440 | tf_op jit(solution)/shard_map/all_gather | solution.py:91
  15.6 233.0 %all-gather.7.cloned.1.call-start = ((), (), s32[]{:S(2)}) async-start(), calls=%async_computation.2 | async-start | bytes 13107200 | tf_op jit(solution)/shard_map/all_gather | solution.py:89
  16.4 363.7 %all-gather.9.cloned.1.call-start = ((), (), s32[]{:S(2)}) async-start(), calls=%async_computation.3 | async-start | bytes 26214400 | tf_op jit(solution)/shard_map/all_gather | solution.py:90
  380.1 4.0 copy-start
  384.1 1.6 copy-start.1
  411.5 28.3 %copy-start.4 = (u32[32]{0:T(128)S(1)}, u32[32]{0:T(128)}, u32[]{:S(2)}) copy-start(u32[32]{0:T(128)} %constant.108) | copy-start | bytes 388
  414.0 52.9 %all-to-all-start = ((f32[4,1,65536]{2,1,0:T(1,128)}), f32[4,1,65536]{2,1,0:T(1,128)S(1)}, u32[]{:S(2)}, u32[]{:S(2)}) async-start(f32[4,1,65536]{2,1,0:T(1,128)} %reshape.307), calls=%async_computation | async-start | bytes 2097152 | tf_op jit(solution)/shard_map/all_to_all | solution.py:111
  472.1 3.9 copy-start.3
  478.3 39.6 %copy-start.2 = (f32[32,64,64]{2,1,0:T(8,128)}, f32[32,64,64]{2,1,0:T(8,128)S(1)}, u32[]{:S(2)}) copy-start(f32[32,64,64]{2,1,0:T(8,128)S(1)} %get-tuple-element.11) | copy-start | bytes 1572868
Sparse Core Ops, SparseCore 0:
  15.8 48.6 all-gather.4
  66.0 182.6 all-gather.6
  250.2 129.7 all-gather.8

commit v2 on v1

v2 whole, which is shorter than its diff:
```python
import functools

import jax
import jax.numpy as jnp
from jax import lax
from jax.experimental import pallas as pl
from jax.experimental.pallas import tpu as pltpu
from jax.sharding import PartitionSpec as P


def peer(index):
    return dict(device_id={"sector": index}, device_id_type=pl.DeviceIdType.MESH)


def gather_kernel(p, q, chunks, left, right, psi, left_all, right_all, psi_all,
                  l_send, l_recv, s_send, s_recv, r_send, r_recv, own_sem):
    device = lax.axis_index("sector")
    z, y = device // q, device % q
    mate = z * q + (y // 2) * 2 + (1 - y % 2)
    across = z * q + (y + 2) % q
    across_y = (y + 2) % q
    n = left.shape[0] // chunks
    rights = right.shape[0]
    has_up, has_down = z + 1 < p, z > 0

    barrier = pltpu.get_barrier_semaphore()
    pl.semaphore_signal(barrier, inc=1, **peer(mate))
    pl.semaphore_signal(barrier, inc=1, **peer(across))

    @pl.when(has_up)
    def _():
        pl.semaphore_signal(barrier, inc=1, **peer(device + q))

    @pl.when(has_down)
    def _():
        pl.semaphore_signal(barrier, inc=1, **peer(device - q))

    pl.semaphore_wait(barrier, 4 - (z + 1) // p - (p - z) // p)

    own = [
        pltpu.make_async_copy(left, left_all.at[z], own_sem.at[0]),
        pltpu.make_async_copy(right, right_all.at[y], own_sem.at[1]),
        pltpu.make_async_copy(psi, psi_all.at[z], own_sem.at[2]),
    ]

    def l_copy(way, t, c, shard):
        part = pl.ds(c * n, n)
        src = left.at[part] if t == 0 else left_all.at[shard, part]
        return pltpu.make_async_remote_copy(
            src, left_all.at[shard, part], l_send.at[way, t, c], l_recv.at[way, t, c],
            **peer(device + (q if way == 0 else -q)))

    def s_copy(way, t, shard):
        src = psi if t == 0 else psi_all.at[shard]
        return pltpu.make_async_remote_copy(
            src, psi_all.at[shard], s_send.at[way, t], s_recv.at[way, t],
            **peer(device + (q if way == 0 else -q)))

    def out_shard(way, t):
        return z - t if way == 0 else z + t

    def sends(way, t):
        return ((z - t >= 0) & has_up) if way == 0 else ((z + t < p) & has_down)

    def in_shard(way, t):
        return z - 1 - t if way == 0 else z + 1 + t

    def gets(way, t):
        return (z - 1 - t >= 0) if way == 0 else (z + 1 + t < p)

    def r_copy(kind, c):
        if kind == 0:
            src, dst, to = right.at[c], right_all.at[y, c], across
        elif kind == 1:
            src, dst, to = right.at[c], right_all.at[y, c], mate
        else:
            src, dst, to = right_all.at[across_y, c], right_all.at[across_y, c], mate
        return pltpu.make_async_remote_copy(
            src, dst, r_send.at[kind, c], r_recv.at[kind, c], **peer(to))

    def r_forward(c):
        r_copy(0, c).wait_recv()
        r_copy(2, c).start()

    merged = p > 3 and 2 * chunks == rights

    for t in range(p):
        if t < p - 1:
            for way in (0, 1):
                if t > 0:
                    @pl.when(gets(way, t - 1))
                    def _(way=way, t=t):
                        s_copy(way, t - 1, in_shard(way, t - 1)).wait_recv()

                @pl.when(sends(way, t))
                def _(way=way, t=t):
                    s_copy(way, t, out_shard(way, t)).start()

        def step(c, carry, t=t):
            for way in (0, 1):
                if t > 0:
                    @pl.when(gets(way, t - 1))
                    def _(way=way):
                        l_copy(way, t - 1, c, in_shard(way, t - 1)).wait_recv()

                if t < p - 1:
                    @pl.when(sends(way, t))
                    def _(way=way):
                        l_copy(way, t, c, out_shard(way, t)).start()
            if t in (1, 2) and merged:
                r_forward((t - 1) * chunks + c)
            return carry

        lax.fori_loop(0, chunks, step, 0)
        if t == 0:
            def first(c, carry):
                r_copy(0, c).start()
                r_copy(1, c).start()
                return carry

            lax.fori_loop(0, rights, first, 0)
            for copy in own:
                copy.start()

    for way in (0, 1):
        @pl.when(gets(way, p - 2))
        def _(way=way):
            s_copy(way, p - 2, in_shard(way, p - 2)).wait_recv()

    if not merged:
        def rest(c, carry):
            r_forward(c)
            return carry

        lax.fori_loop(0, rights, rest, 0)

    def finish(c, carry):
        r_copy(0, c).wait_send()
        r_copy(1, c).wait_send()
        r_copy(2, c).wait_send()
        r_copy(1, c).wait_recv()
        r_copy(2, c).wait_recv()
        return carry

    lax.fori_loop(0, rights, finish, 0)
    for t in range(p - 1):
        for way in (0, 1):
            @pl.when(sends(way, t))
            def _(way=way, t=t):
                s_copy(way, t, out_shard(way, t)).wait_send()

                def drain(c, carry):
                    l_copy(way, t, c, out_shard(way, t)).wait_send()
                    return carry

                lax.fori_loop(0, chunks, drain, 0)
    for copy in own:
        copy.wait()


def gather(p, q, left, right, psi):
    chunks = left.shape[0] if p <= 4 else 2
    anyspace = pl.BlockSpec(memory_space=pl.ANY)
    dma = pltpu.SemaphoreType.DMA
    return pl.pallas_call(
        functools.partial(gather_kernel, p, q, chunks),
        out_shape=(
            jax.ShapeDtypeStruct((p,) + left.shape, left.dtype),
            jax.ShapeDtypeStruct((q,) + right.shape, right.dtype),
            jax.ShapeDtypeStruct((p,) + psi.shape, psi.dtype),
        ),
        in_specs=[anyspace] * 3,
        out_specs=(anyspace,) * 3,
        scratch_shapes=[
            dma((2, p - 1, chunks)), dma((2, p - 1, chunks)),
            dma((2, p - 1)), dma((2, p - 1)),
            dma((3, right.shape[0])), dma((3, right.shape[0])), dma((3,)),
        ],
        compiler_params=pltpu.CompilerParams(collective_id=0, has_side_effects=True),
    )(left, right, psi)


def return_kernel(p, q, out, stat, back, stat_all, send, recv, st_send, st_recv, own_sem):
    device = lax.axis_index("sector")
    owners = p * q
    z, y = device // q, device % q
    barrier = pltpu.get_barrier_semaphore()

    def greet(d, carry):
        pl.semaphore_signal(barrier, inc=1, **peer((device + d) % owners))
        return carry

    lax.fori_loop(1, owners, greet, 0)
    pl.semaphore_wait(barrier, owners - 1)

    def tiles(d):
        to = (z + d) % p
        return pltpu.make_async_remote_copy(
            out.at[to], back.at[z], send.at[d], recv.at[d], **peer(to * q + y))

    def stats(d):
        return pltpu.make_async_remote_copy(
            stat, stat_all.at[device], st_send.at[d], st_recv.at[d],
            **peer((device + d) % owners))

    def each(low, high, act):
        def step(d, carry):
            act(d)
            return carry

        lax.fori_loop(low, high, step, 0)

    own = [
        pltpu.make_async_copy(out.at[z], back.at[z], own_sem.at[0]),
        pltpu.make_async_copy(stat, stat_all.at[device], own_sem.at[1]),
    ]
    each(1, owners, lambda d: stats(d).start())
    each(1, p, lambda d: tiles(d).start())
    for copy in own:
        copy.start()
    each(1, owners, lambda d: stats(d).wait())
    each(1, p, lambda d: tiles(d).wait())
    for copy in own:
        copy.wait()


def give_back(p, q, out, stat):
    anyspace = pl.BlockSpec(memory_space=pl.ANY)
    dma = pltpu.SemaphoreType.DMA
    return pl.pallas_call(
        functools.partial(return_kernel, p, q),
        out_shape=(
            jax.ShapeDtypeStruct(out.shape, out.dtype),
            jax.ShapeDtypeStruct((p * q,) + stat.shape, stat.dtype),
        ),
        in_specs=[anyspace] * 2,
        out_specs=(anyspace,) * 2,
        scratch_shapes=[dma((p,)), dma((p,)), dma((p * q,)), dma((p * q,)), dma((2,))],
        compiler_params=pltpu.CompilerParams(collective_id=1, has_side_effects=True),
    )(out, stat)


def apply_kernel(li, ri, pi, ok, rows, cols, psi0, psi1, l0, l1, r0, r1, out_ref, stat_ref):
    step = pl.program_id(0)
    tile = l0.shape[1]
    wide = 4 * tile
    chunks = l0.shape[2] // wide
    for half, (psi_ref, l_ref, r_ref) in enumerate(((psi0, l0, r0), (psi1, l1, r1))):
        s = step * 2 + half
        lanes = slice(half * tile, (half + 1) * tile)

        @pl.when(ok[s] > 0)
        def _():
            pair = psi_ref[0].astype(jnp.float32)
            psi_f = jnp.where(pi[s] % 2 == 0, pair[:, :tile], pair[:, tile:])
            psi = psi_f.astype(jnp.bfloat16)
            row = jnp.concatenate([psi] * 4, axis=1)
            full = jnp.concatenate([row] * 4, axis=0)
            ia = lax.broadcasted_iota(jnp.int32, (wide, wide), 0) // tile
            ib = lax.broadcasted_iota(jnp.int32, (wide, wide), 1) // tile
            diag = jnp.where(ia == ib, full, jnp.zeros_like(full))
            acc = jnp.zeros((tile, tile), jnp.float32)
            for k in range(chunks):
                cut = slice(k * wide, (k + 1) * wide)
                t = jnp.dot(l_ref[0, :, cut], diag, preferred_element_type=jnp.float32)
                acc += lax.dot_general(
                    t.astype(jnp.bfloat16), r_ref[0, :, cut], (((1,), (1,)), ((), ())),
                    preferred_element_type=jnp.float32,
                )
            a = lax.broadcasted_iota(jnp.int32, (tile, tile), 0)
            e = lax.broadcasted_iota(jnp.int32, (tile, tile), 1)
            acc = jnp.where((a < rows[s]) & (e < cols[s]), acc, 0.0)
            out_ref[0, :, lanes] = acc
            ph = jnp.sum(psi_f * acc, keepdims=True)
            pp = jnp.sum(psi_f * psi_f, keepdims=True)
            th = jnp.where(pp > 0, ph / jnp.where(pp > 0, pp, 1.0), 0.0)
            rest = acc - th * psi_f
            ss = jnp.sum(rest * rest, keepdims=True)
            lane = lax.broadcasted_iota(jnp.int32, (4, 128), 1)
            stat_ref[0, 4 * half:4 * half + 4, :] = jnp.where(
                lane == 0, ph, jnp.where(lane == 1, pp, jnp.where(lane == 2, ss, th)))

        @pl.when(ok[s] == 0)
        def _():
            out_ref[0, :, lanes] = jnp.zeros((tile, tile), jnp.float32)
            stat_ref[0, 4 * half:4 * half + 4, :] = jnp.zeros((4, 128), jnp.float32)


def apply_blocks(li, ri, pi, ok, rows, cols, psi, left, right):
    pairs = li.shape[0] // 2
    tile = left.shape[1]
    width = left.shape[2]

    def spec(shape, which, half, scale=1):
        return pl.BlockSpec((1,) + shape, lambda j, *ids: (ids[which][2 * j + half] // scale, 0, 0))

    return pl.pallas_call(
        apply_kernel,
        grid_spec=pltpu.PrefetchScalarGridSpec(
            num_scalar_prefetch=6,
            grid=(pairs,),
            in_specs=[
                spec((tile, 2 * tile), 2, 0, 2), spec((tile, 2 * tile), 2, 1, 2),
                spec((tile, width), 0, 0), spec((tile, width), 0, 1),
                spec((tile, width), 1, 0), spec((tile, width), 1, 1),
            ],
            out_specs=[
                pl.BlockSpec((1, tile, 2 * tile), lambda j, *ids: (j, 0, 0)),
                pl.BlockSpec((1, 8, 128), lambda j, *ids: (j, 0, 0)),
            ],
        ),
        out_shape=[
            jax.ShapeDtypeStruct((pairs, tile, 2 * tile), jnp.float32),
            jax.ShapeDtypeStruct((pairs, 8, 128), jnp.float32),
        ],
        compiler_params=pltpu.CompilerParams(vmem_limit_bytes=32 * 1024 * 1024),
    )(li, ri, pi, ok, rows, cols, psi, psi, left, left, right, right)


def body(psi_blocks, left_sector, left_dims, right_sector, right_dims, left_env, right_env):
    blocks, tile = psi_blocks.shape[:2]
    left_count = left_env.shape[0]
    right_count = right_env.shape[0]
    owners = lax.axis_size("sector")
    device = lax.axis_index("sector")
    cap = (2 * blocks + owners - 1) // owners
    q = 4
    p = owners // q
    slots = min(q * cap, blocks)
    my_z, my_y = device // q, device % q

    left_local = left_sector - device * left_count
    table = right_sector.reshape(owners, blocks)
    own_sector = lax.dynamic_index_in_dim(table, device, 0, keepdims=False)
    rows = jnp.sum(
        jnp.where(left_local[:, None] == jnp.arange(left_count, dtype=jnp.int32)[None, :],
                  left_dims[None, :], 0), axis=1)
    cols = jnp.sum(
        jnp.where(own_sector[:, None] == jnp.arange(right_dims.shape[0], dtype=jnp.int32)[None, :],
                  right_dims[None, :], 0), axis=1)
    place = jnp.arange(tile, dtype=jnp.int32)
    mask = (place[None, :, None] < rows[:, None, None]) & (
        place[None, None, :] < cols[:, None, None])
    psi_used = jnp.where(mask, psi_blocks, jnp.zeros_like(psi_blocks))
    half = blocks // 2
    packed = psi_used.reshape(half, 2, tile, tile).transpose(0, 2, 1, 3).reshape(half, tile, 2 * tile)
    extra = jnp.pad(jnp.stack([left_local, rows]).astype(jnp.bfloat16),
                    ((0, tile - 2), (0, 2 * tile - blocks)))
    sent = jnp.concatenate([packed, extra[None]], axis=0)

    left_all, right_all, psi_all = gather(p, q, left_env, right_env, sent)
    notes = psi_all[:, half, :2, :blocks].astype(jnp.int32)
    left_all = left_all.reshape(p * left_count, tile, -1)
    right_all = right_all.reshape(q * right_count, tile, -1)
    psi_all = psi_all.reshape(p * (half + 1), tile, 2 * tile)

    line = lax.dynamic_index_in_dim(table.reshape(p, q, blocks), my_y, 1, keepdims=False)
    goal = line // (right_count * q)
    order = jnp.arange(blocks, dtype=jnp.int32)
    same = (goal[:, :, None] == goal[:, None, :]) & (order[None, None, :] < order[None, :, None])
    rank = jnp.sum(same.astype(jnp.int32), axis=2)
    match = (goal[:, None, :] == my_z) & (
        rank[:, None, :] == jnp.arange(slots, dtype=jnp.int32)[None, :, None])

    def pick(values):
        return jnp.sum(jnp.where(match, values, 0), axis=2).reshape(p * slots)

    ok = pick(jnp.ones((p, 1, blocks), jnp.int32))
    base = jnp.arange(p, dtype=jnp.int32)[:, None, None]
    pi = pick(base * (blocks + 2) + order[None, None, :])
    li = pick(base * left_count + notes[:, :1])
    slot_rows = pick(notes[:, 1:])
    local_right = line[:, None, :] - my_z * (q * right_count)
    ri = pick(local_right)
    my_dims = lax.dynamic_slice_in_dim(right_dims, my_z * (q * right_count), q * right_count)
    slot_cols = jnp.sum(
        jnp.where(ri[:, None] == jnp.arange(q * right_count, dtype=jnp.int32)[None, :],
                  my_dims[None, :], 0), axis=1)
    out, stat = apply_blocks(li, ri, pi, ok, slot_rows, slot_cols, psi_all, left_all, right_all)
    wide = -(-(p * slots) // 128) * 128
    stat = stat.reshape(p * slots, 4, 128)[:, 0, :4]
    stat = jnp.pad(stat.T, ((0, 4), (0, wide - p * slots)))
    back, stat_all = give_back(p, q, out.reshape(p, slots // 2, tile, 2 * tile), stat)

    own_rank = lax.dynamic_index_in_dim(rank, my_z, 0, keepdims=False)
    target = (own_sector // (right_count * q)) * slots + own_rank
    got = jnp.take(back.reshape(p * slots // 2, tile, 2 * tile), target // 2, axis=0)
    got = jnp.where((target % 2 == 0)[:, None, None], got[:, :, :tile], got[:, :, tile:])
    hpsi = jnp.where(mask, got, jnp.float32(0.0))

    psi_float = psi_used.astype(jnp.float32)
    theta = jnp.sum(stat_all[:, 0]) / jnp.sum(stat_all[:, 1])
    gap = stat_all[:, 3] - theta
    spread = jnp.sum(stat_all[:, 2] + gap * gap * stat_all[:, 1])
    resid = hpsi - theta * psi_float
    scale = jnp.sqrt(spread / (blocks * owners * tile * tile) + 1e-06)
    return (hpsi, resid / scale, jnp.reshape(theta, (1,)))


def solution(mesh):
    placed = (
        P(("groups", "sector"), None, None),
        P(("groups", "sector")),
        P(("groups", "sector")),
        P("groups"),
        P("groups"),
        P(("groups", "sector"), None, None),
        P(("groups", "sector"), None, None),
    )
    return jax.shard_map(
        body,
        mesh=mesh,
        in_specs=placed,
        out_specs=(
            P(("groups", "sector"), None, None),
            P(("groups", "sector"), None, None),
            P("groups"),
        ),
        check_vma=False,
    )
```

time: 526 us -> 378 us (0.72)
  the two profiles are of different devices: /device:TPU:0 before, /device:TPU:10 now
where the time goes in v2:
time: 378 us; the launch traced here: 376 us
  Pallas kernels  348 us (92%)
  local copies, waits for them, and re-layouts  12.2 us (3%)
  other arithmetic  11.3 us (3%)
  between operations  3.97 us (1%)
    pallas_call x1, Pallas kernels, gather(): pl.pallas_call(functools.partial(gather_kernel, p, q, chunks), out_shape=...  252 us
    pallas_call x1, Pallas kernels, give_back(): pl.pallas_call(functools.partial(return_kernel, p, q), out_shape=(jax.Sha...  61.8 us
    pallas_call x1, Pallas kernels, apply_blocks(): pl.pallas_call(apply_kernel, grid_spec=pltpu.PrefetchScalarGridSpec(num_s...  34.7 us

profile of v2, /device:TPU:10, one launch (start us, length us, event | category | flops | bytes accessed | tf_op | source)
XLA Modules:
  0.0 375.5 jit_solution(2527241638229096232)
XLA Ops:
  0.7 0.8 dynamic_slice.18
  1.4 0.7 convert_bitcast_fusion.1
  2.1 0.7 select_reduce_fusion.7
  2.9 0.8 reshape.381
  3.7 0.8 reshape_reshape.3
  4.5 0.2 convert_reduce_fusion
  4.8 0.9 select_reduce_fusion.6
  5.8 1.4 and_select_fusion.1
  7.2 0.5 copy.21
  7.7 0.2 reshape.383
  8.0 0.7 pad_maximum_fusion.psi
  8.7 251.5 %shard_map.94 = (bf16[4,8,64,2560]{3,2,1,0:T(8,128)(2,1)}, bf16[4,16,64,2560]{3,2,1,0:T(8,128)(2,1)}, bf16[4,17,64,128]{3,2,1,0:T(8,128)(2,1)}) custom-call(bf16[8,64,2560]{2,1,0:T(8,128)(2,1)} %left.1, bf16[16,64,2560]{2,1,0:T(8,128)(2,1)} %right.1, bf16[17,64,128]{2,1,0:T(8,128)(2,1)} %pad_maximum_fusion.psi), custom_call_target="tpu_custom_call" | custom-call | tf_op jit(solution)/shard_map/pallas_call | solution.py:165
  260.2 0.7 bitcast_convert_fusion
  261.0 0.4 select_reduce_fusion.1
  262.1 4.0 %copy-done = bf16[4,8,64,2560]{3,2,1,0:T(8,128)(2,1)S(1)} copy-done((bf16[4,8,64,2560]{3,2,1,0:T(8,128)(2,1)S(1)}, bf16[4,8,64,2560]{3,2,1,0:T(8,128)(2,1)}, u32[]{:S(2)}) %copy-start) | copy-done | bytes 10485784
  266.1 1.2 copy-done.1
  267.3 34.7 %shard_map.95 = (f32[32,64,128]{2,1,0:T(8,128)S(1)}, f32[32,8,128]{2,1,0:T(8,128)S(1)}) custom-call(s32[64]{0:T(128)S(1)} %reshape.384.li, s32[64]{0:T(128)S(1)} %reshape.385.ri, s32[64]{0:T(128)S(1)} %reshape.386.pi, s32[64]{0:T(128)S(1)} %reshape.387.ok, s32[64]{0:T(128)S(1)} %reshape.388.rows, s32[64]{0:T(128)S(1)} %select_reduce_fusion.cols, ...), custom_call_target="tpu_custom_call" | custom-call | tf_op jit(solution)/shard_map/pallas_call | solution.py:297
  302.1 1.0 copy-done.2
  303.1 0.6 pad.9.stat
  303.7 61.8 %shard_map.96 = (f32[4,8,64,128]{3,2,1,0:T(8,128)}, f32[16,8,128]{2,1,0:T(8,128)}) custom-call(f32[4,8,64,128]{3,2,1,0:T(8,128)} %bitcast.61, f32[8,128]{1,0:T(8,128)} %pad.9.stat), custom_call_target="tpu_custom_call" | custom-call | tf_op jit(solution)/shard_map/pallas_call | solution.py:230
  365.5 1.8 gather_fusion
  367.5 1.5 slice_reduce_fusion.1
  370.4 1.6 add_reduce_fusion
  372.7 1.7 subtract_divide_fusion
  (30 shorter events, 1.2 us)
Async XLA Ops:
  262.1 4.0 %copy-start = (bf16[4,8,64,2560]{3,2,1,0:T(8,128)(2,1)S(1)}, bf16[4,8,64,2560]{3,2,1,0:T(8,128)(2,1)}, u32[]{:S(2)}) copy-start(bf16[4,8,64,2560]{3,2,1,0:T(8,128)(2,1)} %get-tuple-element.11) | copy-start | bytes 31457284
  266.1 1.2 copy-start.1
  302.0 1.0 copy-start.2
  303.0 69.7 %copy-start.3 = (bf16[32,64,64]{2,1,0:T(8,128)(2,1)S(1)}, bf16[32,64,64]{2,1,0:T(8,128)(2,1)}, u32[]{:S(2)}) copy-start(bf16[32,64,64]{2,1,0:T(8,128)(2,1)} %param.7) | copy-start | bytes 786436

commit v3 on v2

--- a/solution.py
+++ b/solution.py
@@ -107,18 +107,22 @@
                     @pl.when(sends(way, t))
                     def _(way=way):
                         l_copy(way, t, c, out_shard(way, t)).start()
-            if t in (1, 2) and merged:
+            if merged and t < 2:
+                r_copy(0, t * chunks + c).start()
+                r_copy(1, t * chunks + c).start()
+            if merged and t in (1, 2):
                 r_forward((t - 1) * chunks + c)
             return carry
 
         lax.fori_loop(0, chunks, step, 0)
         if t == 0:
-            def first(c, carry):
-                r_copy(0, c).start()
-                r_copy(1, c).start()
-                return carry
-
-            lax.fori_loop(0, rights, first, 0)
+            if not merged:
+                def first(c, carry):
+                    r_copy(0, c).start()
+                    r_copy(1, c).start()
+                    return carry
+
+                lax.fori_loop(0, rights, first, 0)
             for copy in own:
                 copy.start()
 
@@ -271,19 +275,20 @@
             e = lax.broadcasted_iota(jnp.int32, (tile, tile), 1)
             acc = jnp.where((a < rows[s]) & (e < cols[s]), acc, 0.0)
             out_ref[0, :, lanes] = acc
-            ph = jnp.sum(psi_f * acc, keepdims=True)
-            pp = jnp.sum(psi_f * psi_f, keepdims=True)
+            ph = jnp.sum(psi_f * acc, axis=0, keepdims=True)
+            pp = jnp.sum(psi_f * psi_f, axis=0, keepdims=True)
             th = jnp.where(pp > 0, ph / jnp.where(pp > 0, pp, 1.0), 0.0)
             rest = acc - th * psi_f
-            ss = jnp.sum(rest * rest, keepdims=True)
-            lane = lax.broadcasted_iota(jnp.int32, (4, 128), 1)
-            stat_ref[0, 4 * half:4 * half + 4, :] = jnp.where(
-                lane == 0, ph, jnp.where(lane == 1, pp, jnp.where(lane == 2, ss, th)))
+            ss = jnp.sum(rest * rest, axis=0, keepdims=True)
+            stat_ref[0, 0:1, lanes] = ph
+            stat_ref[0, 1:2, lanes] = pp
+            stat_ref[0, 2:3, lanes] = ss
+            stat_ref[0, 3:4, lanes] = th
 
         @pl.when(ok[s] == 0)
         def _():
             out_ref[0, :, lanes] = jnp.zeros((tile, tile), jnp.float32)
-            stat_ref[0, 4 * half:4 * half + 4, :] = jnp.zeros((4, 128), jnp.float32)
+            stat_ref[0, 0:4, lanes] = jnp.zeros((4, tile), jnp.float32)
 
 
 def apply_blocks(li, ri, pi, ok, rows, cols, psi, left, right):
@@ -306,14 +311,14 @@
             ],
             out_specs=[
                 pl.BlockSpec((1, tile, 2 * tile), lambda j, *ids: (j, 0, 0)),
-                pl.BlockSpec((1, 8, 128), lambda j, *ids: (j, 0, 0)),
+                pl.BlockSpec((1, 4, 2 * tile), lambda j, *ids: (j, 0, 0)),
             ],
         ),
         out_shape=[
             jax.ShapeDtypeStruct((pairs, tile, 2 * tile), jnp.float32),
-            jax.ShapeDtypeStruct((pairs, 8, 128), jnp.float32),
+            jax.ShapeDtypeStruct((pairs, 4, 2 * tile), jnp.float32),
         ],
-        compiler_params=pltpu.CompilerParams(vmem_limit_bytes=32 * 1024 * 1024),
+        compiler_params=pltpu.CompilerParams(vmem_limit_bytes=56 * 1024 * 1024),
     )(li, ri, pi, ok, rows, cols, psi, psi, left, left, right, right)
 
 
@@ -377,9 +382,10 @@
         jnp.where(ri[:, None] == jnp.arange(q * right_count, dtype=jnp.int32)[None, :],
                   my_dims[None, :], 0), axis=1)
     out, stat = apply_blocks(li, ri, pi, ok, slot_rows, slot_cols, psi_all, left_all, right_all)
-    wide = -(-(p * slots) // 128) * 128
-    stat = stat.reshape(p * slots, 4, 128)[:, 0, :4]
-    stat = jnp.pad(stat.T, ((0, 4), (0, wide - p * slots)))
+    ph, pp = jnp.sum(stat[:, 0]), jnp.sum(stat[:, 1])
+    local = jnp.where(pp > 0, ph / jnp.where(pp > 0, pp, 1.0), 0.0)
+    ss = jnp.sum(stat[:, 2] + (stat[:, 3] - local) ** 2 * stat[:, 1])
+    stat = jnp.broadcast_to(jnp.pad(jnp.stack([ph, pp, ss, local]), (0, 4))[:, None], (8, 128))
     back, stat_all = give_back(p, q, out.reshape(p, slots // 2, tile, 2 * tile), stat)
 
     own_rank = lax.dynamic_index_in_dim(rank, my_z, 0, keepdims=False)
@@ -389,6 +395,7 @@
     hpsi = jnp.where(mask, got, jnp.float32(0.0))
 
     psi_float = psi_used.astype(jnp.float32)
+    stat_all = stat_all[:, :4, 0]
     theta = jnp.sum(stat_all[:, 0]) / jnp.sum(stat_all[:, 1])
     gap = stat_all[:, 3] - theta
     spread = jnp.sum(stat_all[:, 2] + gap * gap * stat_all[:, 1])

time: 378 us -> 376 us (level)
  other arithmetic: 11.3 us -> 15.3 us
    pallas_call x1, Pallas kernels: 61.8 us -> 27.8 us  [give_back(): pl.pallas_call(functools.partial(return_kernel, p, q), out_shape=(jax.Sha...]
    pallas_call x1, Pallas kernels: 34.7 us -> 66.7 us  [apply_blocks(): pl.pallas_call(apply_kernel, grid_spec=pltpu.PrefetchScalarGridSpec(num_s...]
    unnamed x10 -> x5, local copies, waits for them, and re-layouts: 6.28 us -> 0.01 us
where the time goes in v3:
time: 376 us
  Pallas kernels  346 us (92%)
  other arithmetic  15.3 us (4%)
  local copies, waits for them, and re-layouts  9.2 us (2%)
  between operations  6 us (2%)
    pallas_call x1, Pallas kernels, gather(): pl.pallas_call(functools.partial(gather_kernel, p, q, chunks), out_shape=...  251 us
    pallas_call x1, Pallas kernels, apply_blocks(): pl.pallas_call(apply_kernel, grid_spec=pltpu.PrefetchScalarGridSpec(num_s...  66.7 us
    pallas_call x1, Pallas kernels, give_back(): pl.pallas_call(functools.partial(return_kernel, p, q), out_shape=(jax.Sha...  27.8 us

profile of v3, /device:TPU:10, one launch (start us, length us, event | category | flops | bytes accessed | tf_op | source)
XLA Modules:
  0.0 376.4 jit_solution(3301998087482198051)
XLA Ops:
  0.7 0.8 dynamic_slice.18
  1.4 0.7 convert_bitcast_fusion.1
  2.1 0.7 select_reduce_fusion.7
  2.9 0.8 reshape.384
  3.7 0.8 reshape_reshape.3
  4.8 0.9 select_reduce_fusion.6
  5.8 1.4 and_select_fusion.1
  8.0 0.7 pad_maximum_fusion.psi
  8.7 251.4 %shard_map.94 = (bf16[4,8,64,2560]{3,2,1,0:T(8,128)(2,1)}, bf16[4,16,64,2560]{3,2,1,0:T(8,128)(2,1)}, bf16[4,17,64,128]{3,2,1,0:T(8,128)(2,1)}) custom-call(bf16[8,64,2560]{2,1,0:T(8,128)(2,1)} %left.1, bf16[16,64,2560]{2,1,0:T(8,128)(2,1)} %right.1, bf16[17,64,128]{2,1,0:T(8,128)(2,1)} %pad_maximum_fusion.psi), custom_call_target="tpu_custom_call" | custom-call | tf_op jit(solution)/shard_map/pallas_call | solution.py:169
  260.1 0.7 bitcast_convert_fusion
  261.3 0.6 reshape.391.rows
  262.0 0.7 select_reduce_fusion.cols
  262.8 0.7 reshape.390.ok
  263.4 0.7 reshape.389.pi
  264.7 66.7 %shard_map.95 = (f32[32,64,128]{2,1,0:T(8,128)}, f32[32,4,128]{2,1,0:T(4,128)}) custom-call(s32[64]{0:T(128)} %reshape.387.li, s32[64]{0:T(128)} %copy-done.1, s32[64]{0:T(128)} %reshape.389.pi, s32[64]{0:T(128)} %reshape.390.ok, s32[64]{0:T(128)} %reshape.391.rows, s32[64]{0:T(128)} %select_reduce_fusion.cols, bf16[68,64,128]{2,1,0:T(8,128)(2,1)} %bitcast.62, ...), custom_call_target="tpu_custom_call" | custom-call | tf_op jit(solution)/shard_map/pallas_call | solution.py:302
  331.4 1.7 slice_reduce_fusion
  335.1 1.6 add_reduce_fusion
  336.8 2.0 select_maximum_fusion
  338.8 0.7 broadcast_in_dim.155.stat
  339.5 27.8 %shard_map.96 = (f32[4,8,64,128]{3,2,1,0:T(8,128)}, f32[16,8,128]{2,1,0:T(8,128)}) custom-call(f32[4,8,64,128]{3,2,1,0:T(8,128)} %bitcast.67, f32[8,128]{1,0:T(8,128)} %broadcast_in_dim.155.stat), custom_call_target="tpu_custom_call" | custom-call | tf_op jit(solution)/shard_map/pallas_call | solution.py:234
  367.3 1.8 gather_fusion
  369.3 0.8 slice.53
  370.2 0.6 slice_reduce_fusion.3
  373.5 1.7 subtract_divide_fusion
  (29 shorter events, 3.3 us)
Async XLA Ops:
  262.0 2.7 copy-start.1
  331.4 42.1 %copy-start = (bf16[32,64,64]{2,1,0:T(8,128)(2,1)S(1)}, bf16[32,64,64]{2,1,0:T(8,128)(2,1)}, u32[]{:S(2)}) copy-start(bf16[32,64,64]{2,1,0:T(8,128)(2,1)} %param.7) | copy-start | bytes 786436

commit v4 on v3

--- a/solution.py
+++ b/solution.py
@@ -245,50 +245,55 @@
 
 
 def apply_kernel(li, ri, pi, ok, rows, cols, psi0, psi1, l0, l1, r0, r1, out_ref, stat_ref):
-    step = pl.program_id(0)
+    s = pl.program_id(0) * 2
     tile = l0.shape[1]
     wide = 4 * tile
     chunks = l0.shape[2] // wide
-    for half, (psi_ref, l_ref, r_ref) in enumerate(((psi0, l0, r0), (psi1, l1, r1))):
-        s = step * 2 + half
-        lanes = slice(half * tile, (half + 1) * tile)
-
-        @pl.when(ok[s] > 0)
-        def _():
+    live = ok[s] + ok[s + 1]
+
+    @pl.when(live > 0)
+    def _():
+        ia = lax.broadcasted_iota(jnp.int32, (wide, wide), 0) // tile
+        ib = lax.broadcasted_iota(jnp.int32, (wide, wide), 1) // tile
+        a = lax.broadcasted_iota(jnp.int32, (tile, tile), 0)
+        e = lax.broadcasted_iota(jnp.int32, (tile, tile), 1)
+        psis, diags = [], []
+        for half, psi_ref in enumerate((psi0, psi1)):
             pair = psi_ref[0].astype(jnp.float32)
-            psi_f = jnp.where(pi[s] % 2 == 0, pair[:, :tile], pair[:, tile:])
+            psi_f = jnp.where(pi[s + half] % 2 == 0, pair[:, :tile], pair[:, tile:])
+            psi_f = jnp.where(ok[s + half] > 0, psi_f, 0.0)
             psi = psi_f.astype(jnp.bfloat16)
             row = jnp.concatenate([psi] * 4, axis=1)
             full = jnp.concatenate([row] * 4, axis=0)
-            ia = lax.broadcasted_iota(jnp.int32, (wide, wide), 0) // tile
-            ib = lax.broadcasted_iota(jnp.int32, (wide, wide), 1) // tile
-            diag = jnp.where(ia == ib, full, jnp.zeros_like(full))
-            acc = jnp.zeros((tile, tile), jnp.float32)
-            for k in range(chunks):
-                cut = slice(k * wide, (k + 1) * wide)
-                t = jnp.dot(l_ref[0, :, cut], diag, preferred_element_type=jnp.float32)
-                acc += lax.dot_general(
-                    t.astype(jnp.bfloat16), r_ref[0, :, cut], (((1,), (1,)), ((), ())),
-                    preferred_element_type=jnp.float32,
-                )
-            a = lax.broadcasted_iota(jnp.int32, (tile, tile), 0)
-            e = lax.broadcasted_iota(jnp.int32, (tile, tile), 1)
-            acc = jnp.where((a < rows[s]) & (e < cols[s]), acc, 0.0)
+            psis.append(psi_f)
+            diags.append(jnp.where(ia == ib, full, jnp.zeros_like(full)))
+        parts = [[], []]
+        for k in range(chunks):
+            cut = slice(k * wide, (k + 1) * wide)
+            for half, l_ref in enumerate((l0, l1)):
+                t = jnp.dot(l_ref[0, :, cut], diags[half], preferred_element_type=jnp.float32)
+                parts[half].append(t.astype(jnp.bfloat16))
+        for half, r_ref in enumerate((r0, r1)):
+            lanes = slice(half * tile, (half + 1) * tile)
+            t = jnp.concatenate(parts[half], axis=1)
+            acc = lax.dot_general(t, r_ref[0], (((1,), (1,)), ((), ())),
+                                  preferred_element_type=jnp.float32)
+            acc = jnp.where((a < rows[s + half]) & (e < cols[s + half]) & (ok[s + half] > 0), acc, 0.0)
+            psi_f = psis[half]
             out_ref[0, :, lanes] = acc
             ph = jnp.sum(psi_f * acc, axis=0, keepdims=True)
             pp = jnp.sum(psi_f * psi_f, axis=0, keepdims=True)
             th = jnp.where(pp > 0, ph / jnp.where(pp > 0, pp, 1.0), 0.0)
             rest = acc - th * psi_f
-            ss = jnp.sum(rest * rest, axis=0, keepdims=True)
             stat_ref[0, 0:1, lanes] = ph
             stat_ref[0, 1:2, lanes] = pp
-            stat_ref[0, 2:3, lanes] = ss
+            stat_ref[0, 2:3, lanes] = jnp.sum(rest * rest, axis=0, keepdims=True)
             stat_ref[0, 3:4, lanes] = th
 
-        @pl.when(ok[s] == 0)
-        def _():
-            out_ref[0, :, lanes] = jnp.zeros((tile, tile), jnp.float32)
-            stat_ref[0, 0:4, lanes] = jnp.zeros((4, tile), jnp.float32)
+    @pl.when(live == 0)
+    def _():
+        out_ref[...] = jnp.zeros_like(out_ref)
+        stat_ref[...] = jnp.zeros_like(stat_ref)
 
 
 def apply_blocks(li, ri, pi, ok, rows, cols, psi, left, right):

time: 376 us -> 348 us (0.926); the launches traced: 376 us -> 342 us
  Pallas kernels: 346 us -> 312 us
    pallas_call x1, Pallas kernels: 66.7 us -> 29.1 us  [apply_blocks(): pl.pallas_call(apply_kernel, grid_spec=pltpu.PrefetchScalarGridSpec(num_s...]
where the time goes in v4:
time: 348 us; the launch traced here: 342 us
  Pallas kernels  312 us (90%)
  other arithmetic  15.3 us (4%)
  local copies, waits for them, and re-layouts  9.2 us (3%)
  between operations  6 us (2%)
    pallas_call x1, Pallas kernels, gather(): pl.pallas_call(functools.partial(gather_kernel, p, q, chunks), out_shape=...  251 us
    pallas_call x1, Pallas kernels, give_back(): pl.pallas_call(functools.partial(return_kernel, p, q), out_shape=(jax.Sha...  31.5 us
    pallas_call x1, Pallas kernels, apply_blocks(): pl.pallas_call(apply_kernel, grid_spec=pltpu.PrefetchScalarGridSpec(num_s...  29.1 us

profile of v4, /device:TPU:10, one launch (start us, length us, event | category | flops | bytes accessed | tf_op | source)
XLA Modules:
  0.0 342.4 jit_solution(7538373137437933444)
XLA Ops:
  0.7 0.8 dynamic_slice.18
  1.4 0.7 convert_bitcast_fusion.1
  2.1 0.7 select_reduce_fusion.7
  2.9 0.8 reshape.384
  3.7 0.8 reshape_reshape.3
  4.8 0.9 select_reduce_fusion.6
  5.8 1.4 and_select_fusion.1
  8.0 0.7 pad_maximum_fusion.psi
  8.7 251.4 %shard_map.94 = (bf16[4,8,64,2560]{3,2,1,0:T(8,128)(2,1)}, bf16[4,16,64,2560]{3,2,1,0:T(8,128)(2,1)}, bf16[4,17,64,128]{3,2,1,0:T(8,128)(2,1)}) custom-call(bf16[8,64,2560]{2,1,0:T(8,128)(2,1)} %left.1, bf16[16,64,2560]{2,1,0:T(8,128)(2,1)} %right.1, bf16[17,64,128]{2,1,0:T(8,128)(2,1)} %pad_maximum_fusion.psi), custom_call_target="tpu_custom_call" | custom-call | tf_op jit(solution)/shard_map/pallas_call | solution.py:169
  260.1 0.7 bitcast_convert_fusion
  261.3 0.6 reshape.391.rows
  262.0 0.7 select_reduce_fusion.cols
  262.8 0.7 reshape.390.ok
  263.4 0.7 reshape.389.pi
  264.7 29.1 %shard_map.95 = (f32[32,64,128]{2,1,0:T(8,128)}, f32[32,4,128]{2,1,0:T(4,128)}) custom-call(s32[64]{0:T(128)} %reshape.387.li, s32[64]{0:T(128)} %copy-done.1, s32[64]{0:T(128)} %reshape.389.pi, s32[64]{0:T(128)} %reshape.390.ok, s32[64]{0:T(128)} %reshape.391.rows, s32[64]{0:T(128)} %select_reduce_fusion.cols, bf16[68,64,128]{2,1,0:T(8,128)(2,1)} %bitcast.62, ...), custom_call_target="tpu_custom_call" | custom-call | tf_op jit(solution)/shard_map/pallas_call | solution.py:307
  293.8 1.7 slice_reduce_fusion
  297.5 1.6 add_reduce_fusion
  299.2 2.0 select_maximum_fusion
  301.2 0.7 broadcast_in_dim.155.stat
  301.9 31.5 %shard_map.96 = (f32[4,8,64,128]{3,2,1,0:T(8,128)}, f32[16,8,128]{2,1,0:T(8,128)}) custom-call(f32[4,8,64,128]{3,2,1,0:T(8,128)} %bitcast.67, f32[8,128]{1,0:T(8,128)} %broadcast_in_dim.155.stat), custom_call_target="tpu_custom_call" | custom-call | tf_op jit(solution)/shard_map/pallas_call | solution.py:234
  333.3 1.8 gather_fusion
  335.3 0.8 slice.53
  336.3 0.6 slice_reduce_fusion.3
  339.5 1.7 subtract_divide_fusion
  (29 shorter events, 3.3 us)
Async XLA Ops:
  262.0 2.7 copy-start.1
  293.8 45.7 %copy-start = (bf16[32,64,64]{2,1,0:T(8,128)(2,1)S(1)}, bf16[32,64,64]{2,1,0:T(8,128)(2,1)}, u32[]{:S(2)}) copy-start(bf16[32,64,64]{2,1,0:T(8,128)(2,1)} %param.7) | copy-start | bytes 786436

commit v5 on v4

--- a/solution.py
+++ b/solution.py
@@ -358,7 +358,9 @@
                     ((0, tile - 2), (0, 2 * tile - blocks)))
     sent = jnp.concatenate([packed, extra[None]], axis=0)
 
-    left_all, right_all, psi_all = gather(p, q, left_env, right_env, sent)
+    left_all, right_all, psi_all = gather(
+        p, q, left_env.reshape(2 * left_count, tile // 2, -1),
+        right_env.reshape(2 * right_count, tile // 2, -1), sent)
     notes = psi_all[:, half, :2, :blocks].astype(jnp.int32)
     left_all = left_all.reshape(p * left_count, tile, -1)
     right_all = right_all.reshape(q * right_count, tile, -1)

time: 348 us -> 351 us (level)
  Pallas kernels: 312 us -> 318 us
where the time goes in v5:
time: 351 us; the launch traced here: 349 us
  Pallas kernels  318 us (91%)
  other arithmetic  15.3 us (4%)
  local copies, waits for them, and re-layouts  9.2 us (3%)
  between operations  6 us (2%)
    pallas_call x1, Pallas kernels, gather(): pl.pallas_call(functools.partial(gather_kernel, p, q, chunks), out_shape=...  253 us
    pallas_call x1, Pallas kernels, give_back(): pl.pallas_call(functools.partial(return_kernel, p, q), out_shape=(jax.Sha...  34.5 us
    pallas_call x1, Pallas kernels, apply_blocks(): pl.pallas_call(apply_kernel, grid_spec=pltpu.PrefetchScalarGridSpec(num_s...  30.2 us

profile of v5, /device:TPU:10, one launch (start us, length us, event | category | flops | bytes accessed | tf_op | source)
XLA Modules:
  0.0 348.6 jit_solution(8345772116922384988)
XLA Ops:
  0.7 0.8 dynamic_slice.18
  1.4 0.7 convert_bitcast_fusion.1
  2.1 0.7 select_reduce_fusion.7
  2.9 0.8 reshape.390
  3.7 0.8 reshape_reshape.3
  4.8 0.9 select_reduce_fusion.6
  5.8 1.4 and_select_fusion.1
  8.0 0.7 pad_maximum_fusion.psi
  8.7 253.4 %shard_map.94 = (bf16[4,16,32,2560]{3,2,1,0:T(8,128)(2,1)}, bf16[4,32,32,2560]{3,2,1,0:T(8,128)(2,1)}, bf16[4,17,64,128]{3,2,1,0:T(8,128)(2,1)}) custom-call(bf16[16,32,2560]{2,1,0:T(8,128)(2,1)} %bitcast.67, bf16[32,32,2560]{2,1,0:T(8,128)(2,1)} %bitcast.64, bf16[17,64,128]{2,1,0:T(8,128)(2,1)} %pad_maximum_fusion.psi), custom_call_target="tpu_custom_call" | custom-call | tf_op jit(solution)/shard_map/pallas_call | solution.py:169
  262.1 0.7 bitcast_convert_fusion
  263.3 0.6 reshape.399.rows
  264.1 0.7 select_reduce_fusion.cols
  264.8 0.7 reshape.398.ok
  265.5 0.7 reshape.397.pi
  266.8 30.2 %shard_map.95 = (f32[32,64,128]{2,1,0:T(8,128)}, f32[32,4,128]{2,1,0:T(4,128)}) custom-call(s32[64]{0:T(128)} %reshape.395.li, s32[64]{0:T(128)} %copy-done.1, s32[64]{0:T(128)} %reshape.397.pi, s32[64]{0:T(128)} %reshape.398.ok, s32[64]{0:T(128)} %reshape.399.rows, s32[64]{0:T(128)} %select_reduce_fusion.cols, bf16[68,64,128]{2,1,0:T(8,128)(2,1)} %bitcast.65, ...), custom_call_target="tpu_custom_call" | custom-call | tf_op jit(solution)/shard_map/pallas_call | solution.py:307
  297.0 1.7 slice_reduce_fusion
  300.7 1.6 add_reduce_fusion
  302.3 2.0 select_maximum_fusion
  304.4 0.7 broadcast_in_dim.155.stat
  305.0 34.5 %shard_map.96 = (f32[4,8,64,128]{3,2,1,0:T(8,128)}, f32[16,8,128]{2,1,0:T(8,128)}) custom-call(f32[4,8,64,128]{3,2,1,0:T(8,128)} %bitcast.71, f32[8,128]{1,0:T(8,128)} %broadcast_in_dim.155.stat), custom_call_target="tpu_custom_call" | custom-call | tf_op jit(solution)/shard_map/pallas_call | solution.py:234
  339.5 1.8 gather_fusion
  341.5 0.8 slice.53
  342.5 0.6 slice_reduce_fusion.3
  345.7 1.7 subtract_divide_fusion
  (29 shorter events, 3.3 us)
Async XLA Ops:
  264.1 2.7 copy-start.1
  297.0 48.8 %copy-start = (bf16[32,64,64]{2,1,0:T(8,128)(2,1)S(1)}, bf16[32,64,64]{2,1,0:T(8,128)(2,1)}, u32[]{:S(2)}) copy-start(bf16[32,64,64]{2,1,0:T(8,128)(2,1)} %param.7) | copy-start | bytes 786436

commit v6 on v4

--- a/solution.py
+++ b/solution.py
@@ -27,20 +27,14 @@
     pl.semaphore_signal(barrier, inc=1, **peer(mate))
     pl.semaphore_signal(barrier, inc=1, **peer(across))
 
-    @pl.when(has_up)
-    def _():
-        pl.semaphore_signal(barrier, inc=1, **peer(device + q))
-
-    @pl.when(has_down)
-    def _():
-        pl.semaphore_signal(barrier, inc=1, **peer(device - q))
-
-    pl.semaphore_wait(barrier, 4 - (z + 1) // p - (p - z) // p)
+    for d in range(1, p):
+        pl.semaphore_signal(barrier, inc=1, **peer(((z + d) % p) * q + y))
+    pl.semaphore_wait(barrier, p + 1)
 
     own = [
         pltpu.make_async_copy(left, left_all.at[z], own_sem.at[0]),
         pltpu.make_async_copy(right, right_all.at[y], own_sem.at[1]),
-        pltpu.make_async_copy(psi, psi_all.at[z], own_sem.at[2]),
+        pltpu.make_async_copy(psi.at[z], psi_all.at[z], own_sem.at[2]),
     ]
 
     def l_copy(way, t, c, shard):
@@ -50,11 +44,10 @@
             src, left_all.at[shard, part], l_send.at[way, t, c], l_recv.at[way, t, c],
             **peer(device + (q if way == 0 else -q)))
 
-    def s_copy(way, t, shard):
-        src = psi if t == 0 else psi_all.at[shard]
+    def s_copy(d):
+        to = (z + d) % p
         return pltpu.make_async_remote_copy(
-            src, psi_all.at[shard], s_send.at[way, t], s_recv.at[way, t],
-            **peer(device + (q if way == 0 else -q)))
+            psi.at[to], psi_all.at[z], s_send.at[d], s_recv.at[d], **peer(to * q + y))
 
     def out_shard(way, t):
         return z - t if way == 0 else z + t
@@ -84,18 +77,9 @@
 
     merged = p > 3 and 2 * chunks == rights
 
+    for d in range(1, p):
+        s_copy(d).start()
     for t in range(p):
-        if t < p - 1:
-            for way in (0, 1):
-                if t > 0:
-                    @pl.when(gets(way, t - 1))
-                    def _(way=way, t=t):
-                        s_copy(way, t - 1, in_shard(way, t - 1)).wait_recv()
-
-                @pl.when(sends(way, t))
-                def _(way=way, t=t):
-                    s_copy(way, t, out_shard(way, t)).start()
-
         def step(c, carry, t=t):
             for way in (0, 1):
                 if t > 0:
@@ -126,10 +110,8 @@
             for copy in own:
                 copy.start()
 
-    for way in (0, 1):
-        @pl.when(gets(way, p - 2))
-        def _(way=way):
-            s_copy(way, p - 2, in_shard(way, p - 2)).wait_recv()
+    for d in range(1, p):
+        s_copy(d).wait()
 
     if not merged:
         def rest(c, carry):
@@ -151,8 +133,6 @@
         for way in (0, 1):
             @pl.when(sends(way, t))
             def _(way=way, t=t):
-                s_copy(way, t, out_shard(way, t)).wait_send()
-
                 def drain(c, carry):
                     l_copy(way, t, c, out_shard(way, t)).wait_send()
                     return carry
@@ -171,13 +151,13 @@
         out_shape=(
             jax.ShapeDtypeStruct((p,) + left.shape, left.dtype),
             jax.ShapeDtypeStruct((q,) + right.shape, right.dtype),
-            jax.ShapeDtypeStruct((p,) + psi.shape, psi.dtype),
+            jax.ShapeDtypeStruct(psi.shape, psi.dtype),
         ),
         in_specs=[anyspace] * 3,
         out_specs=(anyspace,) * 3,
         scratch_shapes=[
             dma((2, p - 1, chunks)), dma((2, p - 1, chunks)),
-            dma((2, p - 1)), dma((2, p - 1)),
+            dma((p,)), dma((p,)),
             dma((3, right.shape[0])), dma((3, right.shape[0])), dma((3,)),
         ],
         compiler_params=pltpu.CompilerParams(collective_id=0, has_side_effects=True),
@@ -352,23 +332,34 @@
     mask = (place[None, :, None] < rows[:, None, None]) & (
         place[None, None, :] < cols[:, None, None])
     psi_used = jnp.where(mask, psi_blocks, jnp.zeros_like(psi_blocks))
-    half = blocks // 2
-    packed = psi_used.reshape(half, 2, tile, tile).transpose(0, 2, 1, 3).reshape(half, tile, 2 * tile)
-    extra = jnp.pad(jnp.stack([left_local, rows]).astype(jnp.bfloat16),
-                    ((0, tile - 2), (0, 2 * tile - blocks)))
-    sent = jnp.concatenate([packed, extra[None]], axis=0)
-
-    left_all, right_all, psi_all = gather(p, q, left_env, right_env, sent)
-    notes = psi_all[:, half, :2, :blocks].astype(jnp.int32)
-    left_all = left_all.reshape(p * left_count, tile, -1)
-    right_all = right_all.reshape(q * right_count, tile, -1)
-    psi_all = psi_all.reshape(p * (half + 1), tile, 2 * tile)
-
     line = lax.dynamic_index_in_dim(table.reshape(p, q, blocks), my_y, 1, keepdims=False)
     goal = line // (right_count * q)
     order = jnp.arange(blocks, dtype=jnp.int32)
     same = (goal[:, :, None] == goal[:, None, :]) & (order[None, None, :] < order[None, :, None])
     rank = jnp.sum(same.astype(jnp.int32), axis=2)
+    half = slots // 2
+    own_goal = lax.dynamic_index_in_dim(goal, my_z, 0, keepdims=False)
+    own_rank = lax.dynamic_index_in_dim(rank, my_z, 0, keepdims=False)
+    spot = jnp.arange(slots, dtype=jnp.int32)
+    mine = (own_goal[None, None, :] == jnp.arange(p, dtype=jnp.int32)[:, None, None]) & (
+        own_rank[None, None, :] == spot[None, :, None])
+
+    def own_pick(values):
+        return jnp.sum(jnp.where(mine, values, 0), axis=2)
+
+    picked = jnp.take(psi_used, own_pick(order).reshape(-1), axis=0)
+    picked = picked.reshape(p, half, 2, tile, tile).transpose(0, 1, 3, 2, 4)
+    picked = picked.reshape(p, half, tile, 2 * tile)
+    extra = jnp.stack([own_pick(left_local), own_pick(rows)], axis=1).astype(jnp.bfloat16)
+    extra = jnp.pad(extra, ((0, 0), (0, tile - 2), (0, 2 * tile - slots)))
+    sent = jnp.concatenate([picked, extra[:, None]], axis=1)
+
+    left_all, right_all, psi_all = gather(p, q, left_env, right_env, sent)
+    notes = psi_all[:, half, :2, :slots].astype(jnp.int32)
+    left_all = left_all.reshape(p * left_count, tile, -1)
+    right_all = right_all.reshape(q * right_count, tile, -1)
+    psi_all = psi_all.reshape(p * (half + 1), tile, 2 * tile)
+
     match = (goal[:, None, :] == my_z) & (
         rank[:, None, :] == jnp.arange(slots, dtype=jnp.int32)[None, :, None])
 
@@ -376,10 +367,10 @@
         return jnp.sum(jnp.where(match, values, 0), axis=2).reshape(p * slots)
 
     ok = pick(jnp.ones((p, 1, blocks), jnp.int32))
-    base = jnp.arange(p, dtype=jnp.int32)[:, None, None]
-    pi = pick(base * (blocks + 2) + order[None, None, :])
-    li = pick(base * left_count + notes[:, :1])
-    slot_rows = pick(notes[:, 1:])
+    base = jnp.arange(p, dtype=jnp.int32)[:, None]
+    pi = (base * (slots + 2) + spot[None]).reshape(p * slots)
+    li = (base * left_count + notes[:, 0]).reshape(p * slots)
+    slot_rows = notes[:, 1].reshape(p * slots)
     local_right = line[:, None, :] - my_z * (q * right_count)
     ri = pick(local_right)
     my_dims = lax.dynamic_slice_in_dim(right_dims, my_z * (q * right_count), q * right_count)

time: 348 us -> 349 us (level); the launches traced: 342 us -> 347 us
  no operation moved by 1% of the time
where the time goes in v6:
time: 349 us; the launch traced here: 347 us
  Pallas kernels  315 us (90%)
  other arithmetic  17.2 us (5%)
  local copies, waits for them, and re-layouts  9.58 us (3%)
  between operations  6.05 us (2%)
    pallas_call x1, Pallas kernels, gather(): pl.pallas_call(functools.partial(gather_kernel, p, q, chunks), out_shape=...  248 us
    pallas_call x1, Pallas kernels, give_back(): pl.pallas_call(functools.partial(return_kernel, p, q), out_shape=(jax.Sha...  34.4 us
    pallas_call x1, Pallas kernels, apply_blocks(): pl.pallas_call(apply_kernel, grid_spec=pltpu.PrefetchScalarGridSpec(num_s...  31.9 us

profile of v6, /device:TPU:10, one launch (start us, length us, event | category | flops | bytes accessed | tf_op | source)
XLA Modules:
  0.0 347.5 jit_solution(9004938465966216814)
XLA Ops:
  0.7 0.8 dynamic_slice.23
  1.4 0.7 broadcast_subtract_fusion.1
  2.1 0.7 select_reduce_fusion.4
  2.9 0.7 add.185.pi
  3.7 0.8 reshape.450
  4.5 0.8 reshape_reshape.3
  5.8 0.7 reshape.455.ok
  6.6 0.7 select_reduce_fusion.cols
  7.3 0.9 select_reduce_fusion.3
  9.0 1.4 and_select_fusion.1
  10.4 0.7 gather_fusion
  11.1 1.3 fusion
  12.9 0.9 pad_maximum_fusion.psi
  13.8 248.4 %shard_map.94 = (bf16[4,8,64,2560]{3,2,1,0:T(8,128)(2,1)}, bf16[4,16,64,2560]{3,2,1,0:T(8,128)(2,1)}, bf16[4,9,64,128]{3,2,1,0:T(8,128)(2,1)}) custom-call(bf16[8,64,2560]{2,1,0:T(8,128)(2,1)} %left.1, bf16[16,64,2560]{2,1,0:T(8,128)(2,1)} %right.1, bf16[4,9,64,128]{3,2,1,0:T(8,128)(2,1)} %pad_maximum_fusion.psi), custom_call_target="tpu_custom_call" | custom-call | tf_op jit(solution)/shard_map/pallas_call | solution.py:149
  262.2 0.7 bitcast_convert_fusion
  264.1 31.9 %shard_map.95 = (f32[32,64,128]{2,1,0:T(8,128)}, f32[32,4,128]{2,1,0:T(4,128)}) custom-call(s32[64]{0:T(128)} %add.181.li, s32[64]{0:T(128)} %copy-done.1, s32[64]{0:T(128)} %add.185.pi, s32[64]{0:T(128)} %reshape.455.ok, s32[64]{0:T(128)} %reshape_squeeze.3.rows, s32[64]{0:T(128)} %select_reduce_fusion.cols, bf16[36,64,128]{2,1,0:T(8,128)(2,1)} %bitcast.65, ...), custom_call_target="tpu_custom_call" | custom-call | tf_op jit(solution)/shard_map/pallas_call | solution.py:287
  296.0 1.6 slice_reduce_fusion
  299.7 1.6 add_reduce_fusion
  301.3 2.0 select_maximum_fusion
  303.3 0.7 broadcast_in_dim.161.stat
  304.0 34.4 %shard_map.96 = (f32[4,8,64,128]{3,2,1,0:T(8,128)}, f32[16,8,128]{2,1,0:T(8,128)}) custom-call(f32[4,8,64,128]{3,2,1,0:T(8,128)} %bitcast.68, f32[8,128]{1,0:T(8,128)} %broadcast_in_dim.161.stat), custom_call_target="tpu_custom_call" | custom-call | tf_op jit(solution)/shard_map/pallas_call | solution.py:214
  338.4 1.8 gather_fusion.1
  340.4 0.8 slice.53
  344.6 1.7 subtract_divide_fusion
  (45 shorter events, 4.8 us)
Async XLA Ops:
  6.6 257.5 %copy-start.1 = (s32[64]{0:T(128)}, s32[64]{0:T(128)S(1)}, u32[]{:S(2)}) copy-start(s32[64]{0:T(128)S(1)} %reshape.454.ri) | copy-start | bytes 772
  264.1 80.5 %copy-start = (bf16[32,64,64]{2,1,0:T(8,128)(2,1)S(1)}, bf16[32,64,64]{2,1,0:T(8,128)(2,1)}, u32[]{:S(2)}) copy-start(bf16[32,64,64]{2,1,0:T(8,128)(2,1)} %param.7) | copy-start | bytes 786436
